TPU v7x, 32 devices: a whole 2x2x4 slice. The times are simulated.
32 devices in a mesh: tile: 8 (over z, y), slab: 4 (over x, core).
Axes of the slice: x: 2, y: 2, z: 4, core: 2. Of those that a mesh axis runs over, the one named last changes fastest.
Arguments:
- incident: float32 [2, 1024, 128], P(None, 'tile'), may hold values from -6 to 6
- target: float32 [2, 1024, 128], P(None, 'tile'), may hold values from -6 to 6
- kernel: float32 [2, 33], replicated, may hold values from -0.25 to 0.25
- phase_screen: float32 [8, 1024, 128], P('slab', 'tile'), may hold values from -1.5 to 1.5
- plane_shift: int32 [8], P('slab'), may hold values from -8 to 8, as said below
- slab_planes: int32 [4], P('slab'), may hold values from 1 to 2, 6 in all
Outputs:
- gradient: float32 [8, 1024, 128], P('slab', 'tile')
Inputs may be any that keep to these rules, and one draw needn't show every extreme that they name: `plane_shift`: some plane's shift is exactly 8 and another plane's is exactly minus 8. `slab_planes`: the counts sum to 6, and some slab has exactly 2 live planes; a slab's live planes are its first ones.
All inputs are finite; a program needn't handle non-finite values. No bound on the sum of `slab_planes` on one device may be relied on, other than what follows from the above.
Results may differ from a plain program's by a relative error of at most 0.0003.
Values sent between devices are 32-bit elements; how exact they have to be, the bound alone decides.
A program may use at most 64 MiB of HBM per device.

v0:
```python
import jax
import jax.numpy as jnp
from jax import lax
from jax.sharding import PartitionSpec as P

TILT_MAX = 8


tap_reach = 16
highest = lax.Precision.HIGHEST


def padded_2(block, sides, width):
    for axis, dim in sides:
        count = lax.axis_size(axis)
        forward = [(i, i + 1) for i in range(count - 1)]
        backward = [(target, source) for source, target in forward]
        low = lax.ppermute(
            lax.slice_in_dim(block, block.shape[dim] - width, None, axis=dim), axis, forward
        )
        high = lax.ppermute(lax.slice_in_dim(block, 0, width, axis=dim), axis, backward)
        block = jnp.concatenate([low, block, high], axis=dim)
    return block


def from_behind(array, axis, by):
    count = lax.axis_size(axis)
    pairs = [(i, i + by) for i in range(count) if 0 <= i + by < count]
    return lax.ppermute(array, axis, pairs)


def tap_values(kernel, offsets, conjugate):
    tap_offsets = jnp.arange(2 * tap_reach + 1, dtype=jnp.int32) - tap_reach
    onehot = (offsets[..., None] == tap_offsets).astype(jnp.float32)
    real_part = jnp.sum(onehot * kernel[0], axis=-1)
    imag_part = jnp.sum(onehot * kernel[1], axis=-1)
    if conjugate:
        imag_part = -imag_part
    return jnp.stack([real_part, imag_part])


def row_matrix(kernel, shift_rows, count_out, count_in, forward):
    margin_rows = (count_in - count_out) // 2
    out_index = jnp.arange(count_out, dtype=jnp.int32)[:, None]
    in_index = jnp.arange(count_in, dtype=jnp.int32)[None, :]
    if forward:
        return tap_values(kernel, in_index - margin_rows - out_index - shift_rows, False)
    return tap_values(kernel, out_index - in_index + margin_rows - shift_rows, True)


def col_matrix(kernel, col_count, forward):
    in_index = jnp.arange(col_count, dtype=jnp.int32)[:, None]
    out_index = jnp.arange(col_count, dtype=jnp.int32)[None, :]
    if forward:
        return tap_values(kernel, in_index - out_index, False)
    return tap_values(kernel, out_index - in_index, True)


def product(left_side, right_side):
    return jnp.dot(left_side, right_side, precision=highest, preferred_element_type=jnp.float32)


def left_apply(matrix, field_in):
    real_part = product(matrix[0], field_in[0]) - product(matrix[1], field_in[1])
    imag_part = product(matrix[0], field_in[1]) + product(matrix[1], field_in[0])
    return jnp.stack([real_part, imag_part])


def right_apply(field_in, matrix):
    real_part = product(field_in[0], matrix[0]) - product(field_in[1], matrix[1])
    imag_part = product(field_in[0], matrix[1]) + product(field_in[1], matrix[0])
    return jnp.stack([real_part, imag_part])


def screen(field_in, phase_rows):
    cosine_part = jnp.cos(phase_rows)
    sine_part = jnp.sin(phase_rows)
    return jnp.stack(
        [
            field_in[0] * cosine_part - field_in[1] * sine_part,
            field_in[0] * sine_part + field_in[1] * cosine_part,
        ]
    )


def unscreen(field_in, phase_rows):
    cosine_part = jnp.cos(phase_rows)
    sine_part = jnp.sin(phase_rows)
    return jnp.stack(
        [
            field_in[0] * cosine_part + field_in[1] * sine_part,
            field_in[1] * cosine_part - field_in[0] * sine_part,
        ]
    )


def local(incident, target, kernel, phase_screen, plane_shift, slab_planes):
    row_count = incident.shape[1]
    col_count = incident.shape[2]
    planes = phase_screen.shape[0]
    margin = tap_reach + TILT_MAX
    slab_count = lax.axis_size("slab")
    slab_rank = lax.axis_index("slab")
    live_count = slab_planes[0]
    col_forward = col_matrix(kernel, col_count, True)
    col_adjoint = col_matrix(kernel, col_count, False)
    forward_rows = [
        row_matrix(kernel, plane_shift[index_plane], row_count, row_count + 2 * margin, True)
        for index_plane in range(planes)
    ]
    adjoint_rows = [
        row_matrix(kernel, plane_shift[index_plane], row_count, row_count + 2 * margin, False)
        for index_plane in range(planes)
    ]
    zero_field = jnp.zeros_like(incident)
    zero_plane = jnp.zeros((row_count, col_count), jnp.float32)

    def forward_slab(current):
        fresh_items = []
        moving = current
        for plane_index in range(planes):
            padded = padded_2(moving, (("tile", 1),), margin)

            def plane_local(padded, plane_index=plane_index):
                spread = right_apply(left_apply(forward_rows[plane_index], padded), col_forward)
                lifted = screen(spread, phase_screen[plane_index])
                kept = jnp.where(
                    plane_index < live_count, lifted, padded[:, margin : margin + row_count]
                )
                return (kept, lifted)

            moving, lifted = plane_local(padded)
            fresh_items.append(lifted)
        return (moving, fresh_items)

    def adjoint_slab(adjoint_seed, saved_fields):
        fresh_items = [zero_plane] * planes
        moving = adjoint_seed
        for plane_index in reversed(range(planes)):
            plane_live = plane_index < live_count

            def before_halo(moving, plane_index=plane_index, plane_live=plane_live):
                lifted = saved_fields[plane_index]
                slope_term = lifted[0] * moving[1] - lifted[1] * moving[0]
                weighted = unscreen(moving, phase_screen[plane_index])
                return (
                    jnp.where(plane_live, weighted, moving),
                    jnp.where(plane_live, slope_term, 0.0),
                )

            weighted, slope_term = before_halo(moving)
            padded = padded_2(weighted, (("tile", 1),), margin)

            def after_halo(padded, plane_index=plane_index, plane_live=plane_live):
                returned = right_apply(left_apply(adjoint_rows[plane_index], padded), col_adjoint)
                return jnp.where(plane_live, returned, padded[:, margin : margin + row_count])

            moving = after_halo(padded)
            fresh_items[plane_index] = slope_term
        return (moving, fresh_items)

    current = incident
    saved_fields = [zero_field] * planes
    moving = incident
    for section_index in range(slab_count):
        active = slab_rank == section_index
        moving, fresh_items = forward_slab(current)
        saved_fields = [
            jnp.where(active, new_item, old_item)
            for new_item, old_item in zip(fresh_items, saved_fields)
        ]
        if section_index + 1 < slab_count:
            current = from_behind(moving, "slab", 1)
    adjoint_seed = moving - target
    gradient = [zero_plane] * planes
    for section_index in reversed(range(slab_count)):
        active = slab_rank == section_index
        moving, fresh_items = adjoint_slab(adjoint_seed, saved_fields)
        gradient = [
            jnp.where(active, new_item, old_item)
            for new_item, old_item in zip(fresh_items, gradient)
        ]
        if section_index > 0:
            adjoint_seed = from_behind(moving, "slab", -1)
    return jnp.stack(gradient)


def solution(mesh):
    placed = (
        P(None, "tile", None),
        P(None, "tile", None),
        P(),
        P("slab", "tile", None),
        P("slab"),
        P("slab"),
    )
    return jax.shard_map(
        local, mesh=mesh, in_specs=placed, out_specs=P("slab", "tile", None), check_vma=False
    )
```

profile of v0, /device:TPU:1, one launch (start us, length us, event | category | flops | bytes accessed | tf_op | source)
XLA Modules:
  0.0 217.8 jit_solution(10704692595646365989)
XLA Ops:
  2.1 4.6 %collective-permute-start = (f32[2,24,128]{2,1,0:T(8,128)S(1)}, f32[2,24,128]{2,1,0:T(8,128)S(1)}, u32[]{:S(2)}, u32[]{:S(2)}) collective-permute-start(f32[2,24,128]{2,1,0:T(8,128)S(1)} %get-tuple-element.88), channel_id=1, source_target_pairs={{0,4},{4,8},{8,12},{12,16},{16,20},{20,24},{24,28},{1,5},{5,9},{9,... | collective-permute-start | bytes 73736 | tf_op jit(solution)/shard_map/ppermute | solution.py:18
  16.7 4.3 %collective-permute-start.2 = (f32[2,24,128]{2,1,0:T(8,128)S(1)}, f32[2,24,128]{2,1,0:T(8,128)S(1)}, u32[]{:S(2)}, u32[]{:S(2)}) collective-permute-start(f32[2,24,128]{2,1,0:T(8,128)S(1)} %get-tuple-element.85), channel_id=1, source_target_pairs={{0,4},{4,8},{8,12},{12,16},{16,20},{20,24},{24,28},{1,5},{5,9},{9,... | collective-permute-start | bytes 73736 | tf_op jit(solution)/shard_map/ppermute | solution.py:18
  22.3 3.3 %collective-permute-done.3 = f32[2,24,128]{2,1,0:T(8,128)S(1)} collective-permute-done((f32[2,24,128]{2,1,0:T(8,128)S(1)}, f32[2,24,128]{2,1,0:T(8,128)S(1)}, u32[]{:S(2)}, u32[]{:S(2)}) %collective-permute-start.3) | collective-permute-done | bytes 24608 | tf_op jit(solution)/shard_map/ppermute | solution.py:21
  28.4 5.7 %collective-permute-start.4 = (f32[2,128,128]{2,1,0:T(8,128)S(1)}, f32[2,128,128]{2,1,0:T(8,128)S(1)}, u32[]{:S(2)}, u32[]{:S(2)}) collective-permute-start(f32[2,128,128]{2,1,0:T(8,128)S(1)} %fusion.31), channel_id=1, source_target_pairs={{0,1},{1,2},{2,3},{4,5},{5,6},{6,7},{8,9},{9,10},{10,11},{12,13},{... | collective-permute-start | bytes 393224 | tf_op jit(solution)/shard_map/ppermute | solution.py:29
  36.0 3.1 %collective-permute-start.5 = (f32[2,24,128]{2,1,0:T(8,128)S(1)}, f32[2,24,128]{2,1,0:T(8,128)S(1)}, u32[]{:S(2)}, u32[]{:S(2)}) collective-permute-start(f32[2,24,128]{2,1,0:T(8,128)S(1)} %get-tuple-element.84), channel_id=1, source_target_pairs={{0,4},{4,8},{8,12},{12,16},{16,20},{20,24},{24,28},{1,5},{5,9},{9,... | collective-permute-start | bytes 73736 | tf_op jit(solution)/shard_map/ppermute | solution.py:18
  40.5 3.2 %collective-permute-done.6 = f32[2,24,128]{2,1,0:T(8,128)S(1)} collective-permute-done((f32[2,24,128]{2,1,0:T(8,128)S(1)}, f32[2,24,128]{2,1,0:T(8,128)S(1)}, u32[]{:S(2)}, u32[]{:S(2)}) %collective-permute-start.6) | collective-permute-done | bytes 24608 | tf_op jit(solution)/shard_map/ppermute | solution.py:21
  46.5 4.0 %collective-permute-start.7 = (f32[2,24,128]{2,1,0:T(8,128)S(1)}, f32[2,24,128]{2,1,0:T(8,128)S(1)}, u32[]{:S(2)}, u32[]{:S(2)}) collective-permute-start(f32[2,24,128]{2,1,0:T(8,128)S(1)} %get-tuple-element.81), channel_id=1, source_target_pairs={{0,4},{4,8},{8,12},{12,16},{16,20},{20,24},{24,28},{1,5},{5,9},{9,... | collective-permute-start | bytes 73736 | tf_op jit(solution)/shard_map/ppermute | solution.py:18
  51.8 3.3 %collective-permute-done.8 = f32[2,24,128]{2,1,0:T(8,128)S(1)} collective-permute-done((f32[2,24,128]{2,1,0:T(8,128)S(1)}, f32[2,24,128]{2,1,0:T(8,128)S(1)}, u32[]{:S(2)}, u32[]{:S(2)}) %collective-permute-start.8) | collective-permute-done | bytes 24608 | tf_op jit(solution)/shard_map/ppermute | solution.py:21
  57.9 7.2 %collective-permute-start.9 = (f32[2,128,128]{2,1,0:T(8,128)S(1)}, f32[2,128,128]{2,1,0:T(8,128)S(1)}, u32[]{:S(2)}, u32[]{:S(2)}) collective-permute-start(f32[2,128,128]{2,1,0:T(8,128)S(1)} %fusion.29), channel_id=1, source_target_pairs={{0,1},{1,2},{2,3},{4,5},{5,6},{6,7},{8,9},{9,10},{10,11},{12,13},{... | collective-permute-start | bytes 393224 | tf_op jit(solution)/shard_map/ppermute | solution.py:29
  67.1 3.1 %collective-permute-start.10 = (f32[2,24,128]{2,1,0:T(8,128)S(1)}, f32[2,24,128]{2,1,0:T(8,128)S(1)}, u32[]{:S(2)}, u32[]{:S(2)}) collective-permute-start(f32[2,24,128]{2,1,0:T(8,128)S(1)} %get-tuple-element.80), channel_id=1, source_target_pairs={{0,4},{4,8},{8,12},{12,16},{16,20},{20,24},{24,28},{1,5},{5,9},{9,... | collective-permute-start | bytes 73736 | tf_op jit(solution)/shard_map/ppermute | solution.py:18
  71.5 3.2 %collective-permute-done.11 = f32[2,24,128]{2,1,0:T(8,128)S(1)} collective-permute-done((f32[2,24,128]{2,1,0:T(8,128)S(1)}, f32[2,24,128]{2,1,0:T(8,128)S(1)}, u32[]{:S(2)}, u32[]{:S(2)}) %collective-permute-start.11) | collective-permute-done | bytes 24608 | tf_op jit(solution)/shard_map/ppermute | solution.py:21
  77.6 4.0 %collective-permute-start.12 = (f32[2,24,128]{2,1,0:T(8,128)S(1)}, f32[2,24,128]{2,1,0:T(8,128)S(1)}, u32[]{:S(2)}, u32[]{:S(2)}) collective-permute-start(f32[2,24,128]{2,1,0:T(8,128)S(1)} %get-tuple-element.77), channel_id=1, source_target_pairs={{0,4},{4,8},{8,12},{12,16},{16,20},{20,24},{24,28},{1,5},{5,9},{9,... | collective-permute-start | bytes 73736 | tf_op jit(solution)/shard_map/ppermute | solution.py:18
  83.1 3.1 %collective-permute-done.13 = f32[2,24,128]{2,1,0:T(8,128)S(1)} collective-permute-done((f32[2,24,128]{2,1,0:T(8,128)S(1)}, f32[2,24,128]{2,1,0:T(8,128)S(1)}, u32[]{:S(2)}, u32[]{:S(2)}) %collective-permute-start.13) | collective-permute-done | bytes 24608 | tf_op jit(solution)/shard_map/ppermute | solution.py:21
  89.0 7.2 %collective-permute-start.14 = (f32[2,128,128]{2,1,0:T(8,128)S(1)}, f32[2,128,128]{2,1,0:T(8,128)S(1)}, u32[]{:S(2)}, u32[]{:S(2)}) collective-permute-start(f32[2,128,128]{2,1,0:T(8,128)S(1)} %fusion.27), channel_id=1, source_target_pairs={{0,1},{1,2},{2,3},{4,5},{5,6},{6,7},{8,9},{9,10},{10,11},{12,13},{... | collective-permute-start | bytes 393224 | tf_op jit(solution)/shard_map/ppermute | solution.py:29
  98.1 3.1 %collective-permute-start.15 = (f32[2,24,128]{2,1,0:T(8,128)S(1)}, f32[2,24,128]{2,1,0:T(8,128)S(1)}, u32[]{:S(2)}, u32[]{:S(2)}) collective-permute-start(f32[2,24,128]{2,1,0:T(8,128)S(1)} %get-tuple-element.76), channel_id=1, source_target_pairs={{0,4},{4,8},{8,12},{12,16},{16,20},{20,24},{24,28},{1,5},{5,9},{9,... | collective-permute-start | bytes 73736 | tf_op jit(solution)/shard_map/ppermute | solution.py:18
  102.6 3.2 %collective-permute-done.16 = f32[2,24,128]{2,1,0:T(8,128)S(1)} collective-permute-done((f32[2,24,128]{2,1,0:T(8,128)S(1)}, f32[2,24,128]{2,1,0:T(8,128)S(1)}, u32[]{:S(2)}, u32[]{:S(2)}) %collective-permute-start.16) | collective-permute-done | bytes 24608 | tf_op jit(solution)/shard_map/ppermute | solution.py:21
  108.7 2.8 %collective-permute-start.17 = (f32[2,24,128]{2,1,0:T(8,128)S(1)}, f32[2,24,128]{2,1,0:T(8,128)S(1)}, u32[]{:S(2)}, u32[]{:S(2)}) collective-permute-start(f32[2,24,128]{2,1,0:T(8,128)S(1)} %get-tuple-element.73), channel_id=1, source_target_pairs={{0,4},{4,8},{8,12},{12,16},{16,20},{20,24},{24,28},{1,5},{5,9},{9,... | collective-permute-start | bytes 73736 | tf_op jit(solution)/shard_map/ppermute | solution.py:18
  112.8 3.3 %collective-permute-done.18 = f32[2,24,128]{2,1,0:T(8,128)S(1)} collective-permute-done((f32[2,24,128]{2,1,0:T(8,128)S(1)}, f32[2,24,128]{2,1,0:T(8,128)S(1)}, u32[]{:S(2)}, u32[]{:S(2)}) %collective-permute-start.18) | collective-permute-done | bytes 24608 | tf_op jit(solution)/shard_map/ppermute | solution.py:21
  119.8 2.8 %collective-permute-start.19 = (f32[2,24,128]{2,1,0:T(8,128)S(1)}, f32[2,24,128]{2,1,0:T(8,128)S(1)}, u32[]{:S(2)}, u32[]{:S(2)}) collective-permute-start(f32[2,24,128]{2,1,0:T(8,128)S(1)} %get-tuple-element.69), channel_id=1, source_target_pairs={{0,4},{4,8},{8,12},{12,16},{16,20},{20,24},{24,28},{1,5},{5,9},{9,... | collective-permute-start | bytes 73736 | tf_op jit(solution)/shard_map/ppermute | solution.py:18
  123.9 3.3 %collective-permute-done.20 = f32[2,24,128]{2,1,0:T(8,128)S(1)} collective-permute-done((f32[2,24,128]{2,1,0:T(8,128)S(1)}, f32[2,24,128]{2,1,0:T(8,128)S(1)}, u32[]{:S(2)}, u32[]{:S(2)}) %collective-permute-start.20) | collective-permute-done | bytes 24608 | tf_op jit(solution)/shard_map/ppermute | solution.py:21
  130.1 2.8 %collective-permute-start.21 = (f32[2,24,128]{2,1,0:T(8,128)S(1)}, f32[2,24,128]{2,1,0:T(8,128)S(1)}, u32[]{:S(2)}, u32[]{:S(2)}) collective-permute-start(f32[2,24,128]{2,1,0:T(8,128)S(1)} %get-tuple-element.67), channel_id=1, source_target_pairs={{0,4},{4,8},{8,12},{12,16},{16,20},{20,24},{24,28},{1,5},{5,9},{9,... | collective-permute-start | bytes 73736 | tf_op jit(solution)/shard_map/ppermute | solution.py:18
  134.3 3.3 %collective-permute-done.22 = f32[2,24,128]{2,1,0:T(8,128)S(1)} collective-permute-done((f32[2,24,128]{2,1,0:T(8,128)S(1)}, f32[2,24,128]{2,1,0:T(8,128)S(1)}, u32[]{:S(2)}, u32[]{:S(2)}) %collective-permute-start.22) | collective-permute-done | bytes 24608 | tf_op jit(solution)/shard_map/ppermute | solution.py:21
  142.1 10.0 %collective-permute-done.23 = f32[2,128,128]{2,1,0:T(8,128)S(1)} collective-permute-done((f32[2,128,128]{2,1,0:T(8,128)S(1)}, f32[2,128,128]{2,1,0:T(8,128)S(1)}, u32[]{:S(2)}, u32[]{:S(2)}) %collective-permute-start.23) | collective-permute-done | bytes 131104 | tf_op jit(solution)/shard_map/ppermute | solution.py:29
  156.3 3.3 %collective-permute-done.25 = f32[2,24,128]{2,1,0:T(8,128)S(1)} collective-permute-done((f32[2,24,128]{2,1,0:T(8,128)S(1)}, f32[2,24,128]{2,1,0:T(8,128)S(1)}, u32[]{:S(2)}, u32[]{:S(2)}) %collective-permute-start.25) | collective-permute-done | bytes 24608 | tf_op jit(solution)/shard_map/ppermute | solution.py:21
  162.6 2.8 %collective-permute-start.26 = (f32[2,24,128]{2,1,0:T(8,128)S(1)}, f32[2,24,128]{2,1,0:T(8,128)S(1)}, u32[]{:S(2)}, u32[]{:S(2)}) collective-permute-start(f32[2,24,128]{2,1,0:T(8,128)S(1)} %get-tuple-element.63), channel_id=1, source_target_pairs={{0,4},{4,8},{8,12},{12,16},{16,20},{20,24},{24,28},{1,5},{5,9},{9,... | collective-permute-start | bytes 73736 | tf_op jit(solution)/shard_map/ppermute | solution.py:18
  166.9 3.0 %collective-permute-done.27 = f32[2,24,128]{2,1,0:T(8,128)S(1)} collective-permute-done((f32[2,24,128]{2,1,0:T(8,128)S(1)}, f32[2,24,128]{2,1,0:T(8,128)S(1)}, u32[]{:S(2)}, u32[]{:S(2)}) %collective-permute-start.27) | collective-permute-done | bytes 24608 | tf_op jit(solution)/shard_map/ppermute | solution.py:21
  174.6 5.0 %collective-permute-done.28 = f32[2,128,128]{2,1,0:T(8,128)S(1)} collective-permute-done((f32[2,128,128]{2,1,0:T(8,128)S(1)}, f32[2,128,128]{2,1,0:T(8,128)S(1)}, u32[]{:S(2)}, u32[]{:S(2)}) %collective-permute-start.28) | collective-permute-done | bytes 131104 | tf_op jit(solution)/shard_map/ppermute | solution.py:29
  183.7 3.3 %collective-permute-done.30 = f32[2,24,128]{2,1,0:T(8,128)S(1)} collective-permute-done((f32[2,24,128]{2,1,0:T(8,128)S(1)}, f32[2,24,128]{2,1,0:T(8,128)S(1)}, u32[]{:S(2)}, u32[]{:S(2)}) %collective-permute-start.30) | collective-permute-done | bytes 24608 | tf_op jit(solution)/shard_map/ppermute | solution.py:21
  189.9 2.8 %collective-permute-start.31 = (f32[2,24,128]{2,1,0:T(8,128)S(1)}, f32[2,24,128]{2,1,0:T(8,128)S(1)}, u32[]{:S(2)}, u32[]{:S(2)}) collective-permute-start(f32[2,24,128]{2,1,0:T(8,128)S(1)} %get-tuple-element.59), channel_id=1, source_target_pairs={{0,4},{4,8},{8,12},{12,16},{16,20},{20,24},{24,28},{1,5},{5,9},{9,... | collective-permute-start | bytes 73736 | tf_op jit(solution)/shard_map/ppermute | solution.py:18
  194.1 3.3 %collective-permute-done.32 = f32[2,24,128]{2,1,0:T(8,128)S(1)} collective-permute-done((f32[2,24,128]{2,1,0:T(8,128)S(1)}, f32[2,24,128]{2,1,0:T(8,128)S(1)}, u32[]{:S(2)}, u32[]{:S(2)}) %collective-permute-start.32) | collective-permute-done | bytes 24608 | tf_op jit(solution)/shard_map/ppermute | solution.py:21
  201.9 5.1 %collective-permute-done.33 = f32[2,128,128]{2,1,0:T(8,128)S(1)} collective-permute-done((f32[2,128,128]{2,1,0:T(8,128)S(1)}, f32[2,128,128]{2,1,0:T(8,128)S(1)}, u32[]{:S(2)}, u32[]{:S(2)}) %collective-permute-start.33) | collective-permute-done | bytes 131104 | tf_op jit(solution)/shard_map/ppermute | solution.py:29
  211.2 3.2 %collective-permute-done.35 = f32[2,24,128]{2,1,0:T(8,128)S(1)} collective-permute-done((f32[2,24,128]{2,1,0:T(8,128)S(1)}, f32[2,24,128]{2,1,0:T(8,128)S(1)}, u32[]{:S(2)}, u32[]{:S(2)}) %collective-permute-start.35) | collective-permute-done | bytes 24608 | tf_op jit(solution)/shard_map/ppermute | solution.py:21
  (249 shorter events, 89.7 us)
Async XLA Ops:
  0.8 12.4 %collective-permute-start.1 = (f32[2,24,128]{2,1,0:T(8,128)S(1)}, f32[2,24,128]{2,1,0:T(8,128)S(1)}, u32[]{:S(2)}, u32[]{:S(2)}) collective-permute-start(f32[2,24,128]{2,1,0:T(8,128)S(1)} %get-tuple-element.87), channel_id=1, source_target_pairs={{4,0},{8,4},{12,8},{16,12},{20,16},{24,20},{28,24},{5,1},{9,5},{13... | collective-permute-start | bytes 73736 | tf_op jit(solution)/shard_map/ppermute | solution.py:21
  2.1 11.1 %collective-permute-start = (f32[2,24,128]{2,1,0:T(8,128)S(1)}, f32[2,24,128]{2,1,0:T(8,128)S(1)}, u32[]{:S(2)}, u32[]{:S(2)}) collective-permute-start(f32[2,24,128]{2,1,0:T(8,128)S(1)} %get-tuple-element.88), channel_id=1, source_target_pairs={{0,4},{4,8},{8,12},{12,16},{16,20},{20,24},{24,28},{1,5},{5,9},{9,... | collective-permute-start | bytes 73736 | tf_op jit(solution)/shard_map/ppermute | solution.py:18
  16.7 5.6 %collective-permute-start.2 = (f32[2,24,128]{2,1,0:T(8,128)S(1)}, f32[2,24,128]{2,1,0:T(8,128)S(1)}, u32[]{:S(2)}, u32[]{:S(2)}) collective-permute-start(f32[2,24,128]{2,1,0:T(8,128)S(1)} %get-tuple-element.85), channel_id=1, source_target_pairs={{0,4},{4,8},{8,12},{12,16},{16,20},{20,24},{24,28},{1,5},{5,9},{9,... | collective-permute-start | bytes 73736 | tf_op jit(solution)/shard_map/ppermute | solution.py:18
  21.0 4.6 %collective-permute-start.3 = (f32[2,24,128]{2,1,0:T(8,128)S(1)}, f32[2,24,128]{2,1,0:T(8,128)S(1)}, u32[]{:S(2)}, u32[]{:S(2)}) collective-permute-start(f32[2,24,128]{2,1,0:T(8,128)S(1)} %get-tuple-element.86), channel_id=1, source_target_pairs={{4,0},{8,4},{12,8},{16,12},{20,16},{24,20},{28,24},{5,1},{9,5},{13... | collective-permute-start | bytes 73736 | tf_op jit(solution)/shard_map/ppermute | solution.py:21
  28.4 7.6 %collective-permute-start.4 = (f32[2,128,128]{2,1,0:T(8,128)S(1)}, f32[2,128,128]{2,1,0:T(8,128)S(1)}, u32[]{:S(2)}, u32[]{:S(2)}) collective-permute-start(f32[2,128,128]{2,1,0:T(8,128)S(1)} %fusion.31), channel_id=1, source_target_pairs={{0,1},{1,2},{2,3},{4,5},{5,6},{6,7},{8,9},{9,10},{10,11},{12,13},{... | collective-permute-start | bytes 393224 | tf_op jit(solution)/shard_map/ppermute | solution.py:29
  36.0 4.4 %collective-permute-start.5 = (f32[2,24,128]{2,1,0:T(8,128)S(1)}, f32[2,24,128]{2,1,0:T(8,128)S(1)}, u32[]{:S(2)}, u32[]{:S(2)}) collective-permute-start(f32[2,24,128]{2,1,0:T(8,128)S(1)} %get-tuple-element.84), channel_id=1, source_target_pairs={{0,4},{4,8},{8,12},{12,16},{16,20},{20,24},{24,28},{1,5},{5,9},{9,... | collective-permute-start | bytes 73736 | tf_op jit(solution)/shard_map/ppermute | solution.py:18
  39.1 4.6 %collective-permute-start.6 = (f32[2,24,128]{2,1,0:T(8,128)S(1)}, f32[2,24,128]{2,1,0:T(8,128)S(1)}, u32[]{:S(2)}, u32[]{:S(2)}) collective-permute-start(f32[2,24,128]{2,1,0:T(8,128)S(1)} %get-tuple-element.83), channel_id=1, source_target_pairs={{4,0},{8,4},{12,8},{16,12},{20,16},{24,20},{28,24},{5,1},{9,5},{13... | collective-permute-start | bytes 73736 | tf_op jit(solution)/shard_map/ppermute | solution.py:21
  46.5 5.4 %collective-permute-start.7 = (f32[2,24,128]{2,1,0:T(8,128)S(1)}, f32[2,24,128]{2,1,0:T(8,128)S(1)}, u32[]{:S(2)}, u32[]{:S(2)}) collective-permute-start(f32[2,24,128]{2,1,0:T(8,128)S(1)} %get-tuple-element.81), channel_id=1, source_target_pairs={{0,4},{4,8},{8,12},{12,16},{16,20},{20,24},{24,28},{1,5},{5,9},{9,... | collective-permute-start | bytes 73736 | tf_op jit(solution)/shard_map/ppermute | solution.py:18
  50.5 4.6 %collective-permute-start.8 = (f32[2,24,128]{2,1,0:T(8,128)S(1)}, f32[2,24,128]{2,1,0:T(8,128)S(1)}, u32[]{:S(2)}, u32[]{:S(2)}) collective-permute-start(f32[2,24,128]{2,1,0:T(8,128)S(1)} %get-tuple-element.82), channel_id=1, source_target_pairs={{4,0},{8,4},{12,8},{16,12},{20,16},{24,20},{28,24},{5,1},{9,5},{13... | collective-permute-start | bytes 73736 | tf_op jit(solution)/shard_map/ppermute | solution.py:21
  57.9 9.1 %collective-permute-start.9 = (f32[2,128,128]{2,1,0:T(8,128)S(1)}, f32[2,128,128]{2,1,0:T(8,128)S(1)}, u32[]{:S(2)}, u32[]{:S(2)}) collective-permute-start(f32[2,128,128]{2,1,0:T(8,128)S(1)} %fusion.29), channel_id=1, source_target_pairs={{0,1},{1,2},{2,3},{4,5},{5,6},{6,7},{8,9},{9,10},{10,11},{12,13},{... | collective-permute-start | bytes 393224 | tf_op jit(solution)/shard_map/ppermute | solution.py:29
  67.1 4.4 %collective-permute-start.10 = (f32[2,24,128]{2,1,0:T(8,128)S(1)}, f32[2,24,128]{2,1,0:T(8,128)S(1)}, u32[]{:S(2)}, u32[]{:S(2)}) collective-permute-start(f32[2,24,128]{2,1,0:T(8,128)S(1)} %get-tuple-element.80), channel_id=1, source_target_pairs={{0,4},{4,8},{8,12},{12,16},{16,20},{20,24},{24,28},{1,5},{5,9},{9,... | collective-permute-start | bytes 73736 | tf_op jit(solution)/shard_map/ppermute | solution.py:18
  70.2 4.6 %collective-permute-start.11 = (f32[2,24,128]{2,1,0:T(8,128)S(1)}, f32[2,24,128]{2,1,0:T(8,128)S(1)}, u32[]{:S(2)}, u32[]{:S(2)}) collective-permute-start(f32[2,24,128]{2,1,0:T(8,128)S(1)} %get-tuple-element.79), channel_id=1, source_target_pairs={{4,0},{8,4},{12,8},{16,12},{20,16},{24,20},{28,24},{5,1},{9,5},{13... | collective-permute-start | bytes 73736 | tf_op jit(solution)/shard_map/ppermute | solution.py:21
  77.6 5.5 %collective-permute-start.12 = (f32[2,24,128]{2,1,0:T(8,128)S(1)}, f32[2,24,128]{2,1,0:T(8,128)S(1)}, u32[]{:S(2)}, u32[]{:S(2)}) collective-permute-start(f32[2,24,128]{2,1,0:T(8,128)S(1)} %get-tuple-element.77), channel_id=1, source_target_pairs={{0,4},{4,8},{8,12},{12,16},{16,20},{20,24},{24,28},{1,5},{5,9},{9,... | collective-permute-start | bytes 73736 | tf_op jit(solution)/shard_map/ppermute | solution.py:18
  81.6 4.6 %collective-permute-start.13 = (f32[2,24,128]{2,1,0:T(8,128)S(1)}, f32[2,24,128]{2,1,0:T(8,128)S(1)}, u32[]{:S(2)}, u32[]{:S(2)}) collective-permute-start(f32[2,24,128]{2,1,0:T(8,128)S(1)} %get-tuple-element.78), channel_id=1, source_target_pairs={{4,0},{8,4},{12,8},{16,12},{20,16},{24,20},{28,24},{5,1},{9,5},{13... | collective-permute-start | bytes 73736 | tf_op jit(solution)/shard_map/ppermute | solution.py:21
  89.0 9.1 %collective-permute-start.14 = (f32[2,128,128]{2,1,0:T(8,128)S(1)}, f32[2,128,128]{2,1,0:T(8,128)S(1)}, u32[]{:S(2)}, u32[]{:S(2)}) collective-permute-start(f32[2,128,128]{2,1,0:T(8,128)S(1)} %fusion.27), channel_id=1, source_target_pairs={{0,1},{1,2},{2,3},{4,5},{5,6},{6,7},{8,9},{9,10},{10,11},{12,13},{... | collective-permute-start | bytes 393224 | tf_op jit(solution)/shard_map/ppermute | solution.py:29
  98.1 4.5 %collective-permute-start.15 = (f32[2,24,128]{2,1,0:T(8,128)S(1)}, f32[2,24,128]{2,1,0:T(8,128)S(1)}, u32[]{:S(2)}, u32[]{:S(2)}) collective-permute-start(f32[2,24,128]{2,1,0:T(8,128)S(1)} %get-tuple-element.76), channel_id=1, source_target_pairs={{0,4},{4,8},{8,12},{12,16},{16,20},{20,24},{24,28},{1,5},{5,9},{9,... | collective-permute-start | bytes 73736 | tf_op jit(solution)/shard_map/ppermute | solution.py:18
  101.3 4.6 %collective-permute-start.16 = (f32[2,24,128]{2,1,0:T(8,128)S(1)}, f32[2,24,128]{2,1,0:T(8,128)S(1)}, u32[]{:S(2)}, u32[]{:S(2)}) collective-permute-start(f32[2,24,128]{2,1,0:T(8,128)S(1)} %get-tuple-element.75), channel_id=1, source_target_pairs={{4,0},{8,4},{12,8},{16,12},{20,16},{24,20},{28,24},{5,1},{9,5},{13... | collective-permute-start | bytes 73736 | tf_op jit(solution)/shard_map/ppermute | solution.py:21
  111.5 4.6 %collective-permute-start.18 = (f32[2,24,128]{2,1,0:T(8,128)S(1)}, f32[2,24,128]{2,1,0:T(8,128)S(1)}, u32[]{:S(2)}, u32[]{:S(2)}) collective-permute-start(f32[2,24,128]{2,1,0:T(8,128)S(1)} %get-tuple-element.74), channel_id=1, source_target_pairs={{4,0},{8,4},{12,8},{16,12},{20,16},{24,20},{28,24},{5,1},{9,5},{13... | collective-permute-start | bytes 73736 | tf_op jit(solution)/shard_map/ppermute | solution.py:21
  119.8 4.1 %collective-permute-start.19 = (f32[2,24,128]{2,1,0:T(8,128)S(1)}, f32[2,24,128]{2,1,0:T(8,128)S(1)}, u32[]{:S(2)}, u32[]{:S(2)}) collective-permute-start(f32[2,24,128]{2,1,0:T(8,128)S(1)} %get-tuple-element.69), channel_id=1, source_target_pairs={{0,4},{4,8},{8,12},{12,16},{16,20},{20,24},{24,28},{1,5},{5,9},{9,... | collective-permute-start | bytes 73736 | tf_op jit(solution)/shard_map/ppermute | solution.py:18
  122.6 4.6 %collective-permute-start.20 = (f32[2,24,128]{2,1,0:T(8,128)S(1)}, f32[2,24,128]{2,1,0:T(8,128)S(1)}, u32[]{:S(2)}, u32[]{:S(2)}) collective-permute-start(f32[2,24,128]{2,1,0:T(8,128)S(1)} %get-tuple-element.70), channel_id=1, source_target_pairs={{4,0},{8,4},{12,8},{16,12},{20,16},{24,20},{28,24},{5,1},{9,5},{13... | collective-permute-start | bytes 73736 | tf_op jit(solution)/shard_map/ppermute | solution.py:21
  130.1 4.1 %collective-permute-start.21 = (f32[2,24,128]{2,1,0:T(8,128)S(1)}, f32[2,24,128]{2,1,0:T(8,128)S(1)}, u32[]{:S(2)}, u32[]{:S(2)}) collective-permute-start(f32[2,24,128]{2,1,0:T(8,128)S(1)} %get-tuple-element.67), channel_id=1, source_target_pairs={{0,4},{4,8},{8,12},{12,16},{16,20},{20,24},{24,28},{1,5},{5,9},{9,... | collective-permute-start | bytes 73736 | tf_op jit(solution)/shard_map/ppermute | solution.py:18
  133.0 4.6 %collective-permute-start.22 = (f32[2,24,128]{2,1,0:T(8,128)S(1)}, f32[2,24,128]{2,1,0:T(8,128)S(1)}, u32[]{:S(2)}, u32[]{:S(2)}) collective-permute-start(f32[2,24,128]{2,1,0:T(8,128)S(1)} %get-tuple-element.68), channel_id=1, source_target_pairs={{4,0},{8,4},{12,8},{16,12},{20,16},{24,20},{28,24},{5,1},{9,5},{13... | collective-permute-start | bytes 73736 | tf_op jit(solution)/shard_map/ppermute | solution.py:21
  140.2 12.0 %collective-permute-start.23 = (f32[2,128,128]{2,1,0:T(8,128)S(1)}, f32[2,128,128]{2,1,0:T(8,128)S(1)}, u32[]{:S(2)}, u32[]{:S(2)}) collective-permute-start(f32[2,128,128]{2,1,0:T(8,128)S(1)} %maximum_select_fusion.3), channel_id=1, source_target_pairs={{1,0},{2,1},{3,2},{5,4},{6,5},{7,6},{9,8},{10,9},{11,10},{13,12},{... | collective-permute-start | bytes 393224 | tf_op jit(solution)/shard_map/ppermute | solution.py:29
  155.0 4.6 %collective-permute-start.25 = (f32[2,24,128]{2,1,0:T(8,128)S(1)}, f32[2,24,128]{2,1,0:T(8,128)S(1)}, u32[]{:S(2)}, u32[]{:S(2)}) collective-permute-start(f32[2,24,128]{2,1,0:T(8,128)S(1)} %get-tuple-element.66), channel_id=1, source_target_pairs={{4,0},{8,4},{12,8},{16,12},{20,16},{24,20},{28,24},{5,1},{9,5},{13... | collective-permute-start | bytes 73736 | tf_op jit(solution)/shard_map/ppermute | solution.py:21
  162.6 4.3 %collective-permute-start.26 = (f32[2,24,128]{2,1,0:T(8,128)S(1)}, f32[2,24,128]{2,1,0:T(8,128)S(1)}, u32[]{:S(2)}, u32[]{:S(2)}) collective-permute-start(f32[2,24,128]{2,1,0:T(8,128)S(1)} %get-tuple-element.63), channel_id=1, source_target_pairs={{0,4},{4,8},{8,12},{12,16},{16,20},{20,24},{24,28},{1,5},{5,9},{9,... | collective-permute-start | bytes 73736 | tf_op jit(solution)/shard_map/ppermute | solution.py:18
  165.4 4.6 %collective-permute-start.27 = (f32[2,24,128]{2,1,0:T(8,128)S(1)}, f32[2,24,128]{2,1,0:T(8,128)S(1)}, u32[]{:S(2)}, u32[]{:S(2)}) collective-permute-start(f32[2,24,128]{2,1,0:T(8,128)S(1)} %get-tuple-element.64), channel_id=1, source_target_pairs={{4,0},{8,4},{12,8},{16,12},{20,16},{24,20},{28,24},{5,1},{9,5},{13... | collective-permute-start | bytes 73736 | tf_op jit(solution)/shard_map/ppermute | solution.py:21
  172.6 6.9 %collective-permute-start.28 = (f32[2,128,128]{2,1,0:T(8,128)S(1)}, f32[2,128,128]{2,1,0:T(8,128)S(1)}, u32[]{:S(2)}, u32[]{:S(2)}) collective-permute-start(f32[2,128,128]{2,1,0:T(8,128)S(1)} %maximum_select_fusion.7), channel_id=1, source_target_pairs={{1,0},{2,1},{3,2},{5,4},{6,5},{7,6},{9,8},{10,9},{11,10},{13,12},{... | collective-permute-start | bytes 393224 | tf_op jit(solution)/shard_map/ppermute | solution.py:29
  182.4 4.6 %collective-permute-start.30 = (f32[2,24,128]{2,1,0:T(8,128)S(1)}, f32[2,24,128]{2,1,0:T(8,128)S(1)}, u32[]{:S(2)}, u32[]{:S(2)}) collective-permute-start(f32[2,24,128]{2,1,0:T(8,128)S(1)} %get-tuple-element.62), channel_id=1, source_target_pairs={{4,0},{8,4},{12,8},{16,12},{20,16},{24,20},{28,24},{5,1},{9,5},{13... | collective-permute-start | bytes 73736 | tf_op jit(solution)/shard_map/ppermute | solution.py:21
  189.9 4.1 %collective-permute-start.31 = (f32[2,24,128]{2,1,0:T(8,128)S(1)}, f32[2,24,128]{2,1,0:T(8,128)S(1)}, u32[]{:S(2)}, u32[]{:S(2)}) collective-permute-start(f32[2,24,128]{2,1,0:T(8,128)S(1)} %get-tuple-element.59), channel_id=1, source_target_pairs={{0,4},{4,8},{8,12},{12,16},{16,20},{20,24},{24,28},{1,5},{5,9},{9,... | collective-permute-start | bytes 73736 | tf_op jit(solution)/shard_map/ppermute | solution.py:18
  192.8 4.6 %collective-permute-start.32 = (f32[2,24,128]{2,1,0:T(8,128)S(1)}, f32[2,24,128]{2,1,0:T(8,128)S(1)}, u32[]{:S(2)}, u32[]{:S(2)}) collective-permute-start(f32[2,24,128]{2,1,0:T(8,128)S(1)} %get-tuple-element.60), channel_id=1, source_target_pairs={{4,0},{8,4},{12,8},{16,12},{20,16},{24,20},{28,24},{5,1},{9,5},{13... | collective-permute-start | bytes 73736 | tf_op jit(solution)/shard_map/ppermute | solution.py:21
  200.0 7.0 %collective-permute-start.33 = (f32[2,128,128]{2,1,0:T(8,128)S(1)}, f32[2,128,128]{2,1,0:T(8,128)S(1)}, u32[]{:S(2)}, u32[]{:S(2)}) collective-permute-start(f32[2,128,128]{2,1,0:T(8,128)S(1)} %maximum_select_fusion.11), channel_id=1, source_target_pairs={{1,0},{2,1},{3,2},{5,4},{6,5},{7,6},{9,8},{10,9},{11,10},{13,12},{... | collective-permute-start | bytes 393224 | tf_op jit(solution)/shard_map/ppermute | solution.py:29
  209.9 4.6 %collective-permute-start.35 = (f32[2,24,128]{2,1,0:T(8,128)S(1)}, f32[2,24,128]{2,1,0:T(8,128)S(1)}, u32[]{:S(2)}, u32[]{:S(2)}) collective-permute-start(f32[2,24,128]{2,1,0:T(8,128)S(1)} %get-tuple-element.58), channel_id=1, source_target_pairs={{4,0},{8,4},{12,8},{16,12},{20,16},{24,20},{28,24},{5,1},{9,5},{13... | collective-permute-start | bytes 73736 | tf_op jit(solution)/shard_map/ppermute | solution.py:21
  (9 other events, 32.5 us)
where the time goes:
time: 219 us; the launch traced here: 218 us
  starting transfers between devices  93.7 us (43%)
  waiting for transfers between devices  71 us (32%)
  matrix products  39.4 us (18%)
  other arithmetic  8.58 us (4%)
  local copies, waits for them, and re-layouts  2.77 us (1%)
  between operations  2.36 us (1%)
    ppermute x15, starting transfers between devices, padded_2(): lax.ppermute(lax.slice_in_dim(block, block.shape[dim] - width, None, axis...  48.1 us
    ppermute x15, waiting for transfers between devices, padded_2(): lax.ppermute(lax.slice_in_dim(block, 0, width, axis=dim), axis, backward)  45.1 us
    dot_general x120, matrix products, product(): jnp.dot(left_side, right_side, precision=highest, preferred_element_type=...  39.4 us
    ppermute x6, waiting for transfers between devices, from_behind(): return lax.ppermute(array, axis, pairs)  25.9 us
    ppermute x6, starting transfers between devices, from_behind(): return lax.ppermute(array, axis, pairs)  25.8 us
    ppermute x15, starting transfers between devices, padded_2(): lax.ppermute(lax.slice_in_dim(block, 0, width, axis=dim), axis, backward)  19.8 us
  transfers between devices with their start and end apart: 36, of which 20 were waited for; matrix products, arithmetic and copies ran while one was open for 3% of the time, Pallas kernels for 0%

commit v1 on v0

v1 whole, which is shorter than its diff:
```python
import functools
import math

import jax
import jax.numpy as jnp
from jax import lax
from jax.experimental import pallas as pl
from jax.experimental.pallas import tpu as pltpu
from jax.sharding import PartitionSpec as P

TILT_MAX = 8
REACH = 16
STEP = REACH + TILT_MAX
DEPTH = 3
MESH = pl.DeviceIdType.MESH
F32, BF16 = jnp.float32, jnp.bfloat16


def groups_of(count):
    out = [DEPTH] * (count // DEPTH)
    if count % DEPTH:
        out.append(count % DEPTH)
    return out


def split(value):
    high = value.astype(BF16)
    return high, (value - high.astype(F32)).astype(BF16)


def dot3(left, right):
    (lh, ll), (rh, rl) = left, right
    go = functools.partial(jnp.dot, preferred_element_type=F32)
    return go(lh, rh) + (go(lh, rl) + go(ll, rh))


def sin_cos(x):
    y = x * x
    sine, cosine = 0.0, 0.0
    for n in (13, 11, 9, 7, 5, 3, 1):
        sine = sine * y + (-1.0) ** (n // 2) / math.factorial(n)
    for n in (14, 12, 10, 8, 6, 4, 2, 0):
        cosine = cosine * y + (-1.0) ** (n // 2) / math.factorial(n)
    return sine * x, cosine


def body(cfg, taps, shifts, counts, incident, target, phases, out, *scratch):
    tiles, slabs, planes, rows, cols, live, fwd, bwd = cfg
    n_ex = len(fwd) + len(bwd)
    (row_m, col_m, ph, par, par_s, sines, cosines, saved, aim, mid, grads,
     own_sem, par_ssem, par_rsem, ph_ssem, ph_rsem, ex_ssem, ex_rsem, g_ssem, g_rsem,
     *fields) = scratch
    edge = ph.shape[2] - rows
    edge //= 2
    tile, slab = lax.axis_index("tile"), lax.axis_index("slab")
    worker = slab == 0
    has_low, has_high = tile > 0, tile < tiles - 1
    barrier = pltpu.get_barrier_semaphore()

    def greet(t, s):
        pl.semaphore_signal(barrier, inc=1, device_id={"tile": t, "slab": s}, device_id_type=MESH)

    @pl.when(worker)
    def _():
        for s in range(1, slabs):
            greet(tile, s)

        @pl.when(has_low)
        def _():
            for s in range(slabs):
                greet(tile - 1, s)

        @pl.when(has_high)
        def _():
            for s in range(slabs):
                greet(tile + 1, s)

    @pl.when(jnp.logical_not(worker))
    def _():
        greet(tile, 0)

    def remote(src, dst, ssem, rsem, t, s):
        return pltpu.make_async_remote_copy(
            src_ref=src, dst_ref=dst, send_sem=ssem, recv_sem=rsem,
            device_id={"tile": t, "slab": s}, device_id_type=MESH)

    def inc_up():
        h = fwd[0] * STEP
        return remote(incident.at[:, rows - h:, :], fields[0].at[:, 0:h, :],
                      ex_ssem.at[0], ex_rsem.at[0], tile + 1, 0)

    def inc_down():
        h = fwd[0] * STEP
        return remote(incident.at[:, 0:h, :], fields[0].at[:, h + rows:, :],
                      ex_ssem.at[1], ex_rsem.at[1], tile - 1, 0)

    def halo_up(e, h):
        return remote(fields[e].at[:, rows:rows + h, :], fields[e].at[:, 0:h, :],
                      ex_ssem.at[2 * e], ex_rsem.at[2 * e], tile + 1, 0)

    def halo_down(e, h):
        return remote(fields[e].at[:, h:2 * h, :], fields[e].at[:, h + rows:, :],
                      ex_ssem.at[2 * e + 1], ex_rsem.at[2 * e + 1], tile - 1, 0)

    def ph_mid(s):
        return remote(phases, ph.at[s, :, edge:edge + rows, :],
                      ph_ssem.at[0], ph_rsem.at[s, 0], tile, 0)

    def ph_up(s):
        return remote(phases.at[:, rows - edge:, :], ph.at[s, :, 0:edge, :],
                      ph_ssem.at[1], ph_rsem.at[s, 1], tile + 1, 0)

    def ph_down(s):
        return remote(phases.at[:, 0:edge, :], ph.at[s, :, edge + rows:, :],
                      ph_ssem.at[2], ph_rsem.at[s, 2], tile - 1, 0)

    def par_send(s):
        return remote(par.at[s], par.at[s], par_ssem, par_rsem.at[s], tile, 0)

    def grad_send(s):
        return remote(grads.at[s], out, g_ssem.at[s], g_rsem, tile, s)

    lane = lax.broadcasted_iota(jnp.int32, (8, cols), 1)
    own = jnp.where(lane == planes, counts[0], 0)
    for i in range(planes):
        own = jnp.where(lane == i, shifts[i], own)
    par[slab] = own

    h0 = fwd[0] * STEP
    local_inc = pltpu.make_async_copy(incident, fields[0].at[:, h0:h0 + rows, :], own_sem.at[0])
    local_ph = pltpu.make_async_copy(phases, ph.at[0, :, edge:edge + rows, :], own_sem.at[1])
    local_aim = pltpu.make_async_copy(target, aim, own_sem.at[2])
    local_par = pltpu.make_async_copy(par, par_s, own_sem.at[3])

    greeters = has_low.astype(jnp.int32) + has_high.astype(jnp.int32)
    pl.semaphore_wait(barrier, greeters + jnp.where(worker, slabs - 1, 1))

    @pl.when(worker & has_high)
    def _():
        inc_up().start()

    @pl.when(worker & has_low)
    def _():
        inc_down().start()

    @pl.when(jnp.logical_not(worker))
    def _():
        par_send(slab).start()
        ph_mid(slab).start()

    if edge:
        @pl.when(has_high)
        def _():
            ph_up(slab).start()

        @pl.when(has_low)
        def _():
            ph_down(slab).start()

    @pl.when(worker)
    def _():
        local_inc.start()
        local_ph.start()
        local_aim.start()

        def clear(has, low):
            @pl.when(jnp.logical_not(has))
            def _():
                for e, size in enumerate(fwd + bwd):
                    h = size * STEP
                    at = slice(0, h) if low else slice(h + rows, 2 * h + rows)
                    fields[e][:, at, :] = jnp.zeros((2, h, cols), F32)
                if edge:
                    at = slice(0, edge) if low else slice(edge + rows, 2 * edge + rows)
                    ph[:, :, at, :] = jnp.zeros((slabs, planes, edge, cols), F32)
        clear(has_low, True)
        clear(has_high, False)

        big, wide = row_m.shape[3:]

        def build(direction):
            sign = 1.0 if direction == 0 else -1.0
            at_row = lax.broadcasted_iota(jnp.int32, (8, wide), 1)
            at_col = lax.broadcasted_iota(jnp.int32, (8, cols), 1)
            band_r = [jnp.zeros((8, wide), F32)] * 2
            band_c = [jnp.zeros((8, cols), F32)] * 2
            for j in range(2 * REACH + 1):
                tap = j if direction == 0 else 2 * REACH - j
                off = REACH - j if direction == 0 else j - REACH
                off %= cols
                here, there = at_row == j, at_col == off
                for part in range(2):
                    gain = 1.0 if part == 0 else sign
                    band_r[part] = jnp.where(here, gain * taps[part, tap], band_r[part])
                    band_c[part] = jnp.where(there, gain * taps[part, j], band_c[part])
            for part in range(2):
                full = jnp.concatenate([band_r[part]] * (big // 8), axis=0)
                full = pltpu.roll(full, 0, 1, stride=1, stride_axis=0)
                row_m[direction, 0, part], row_m[direction, 1, part] = split(full)
            near = jnp.abs(lax.broadcasted_iota(jnp.int32, (cols, cols), 0)
                           - lax.broadcasted_iota(jnp.int32, (cols, cols), 1)) <= REACH
            real, imag = [
                jnp.where(near, pltpu.roll(jnp.concatenate([band_c[part]] * (cols // 8), axis=0),
                                           0, 1, stride=1, stride_axis=0), 0.0)
                for part in range(2)]
            block = jnp.concatenate([jnp.concatenate([real, imag], axis=1),
                                     jnp.concatenate([-imag, real], axis=1)], axis=0)
            col_m[direction, 0], col_m[direction, 1] = split(block)

        build(0)

        def spread(ref, start, count, direction):
            taken = count + 2 * REACH
            field = jnp.concatenate(
                [ref[0, pl.ds(start, taken), :], ref[1, pl.ds(start, taken), :]], axis=1)
            high, low = split(field)
            if taken < wide:
                rest = jnp.zeros((wide - taken, 2 * cols), BF16)
                high = jnp.concatenate([high, rest], axis=0)
                low = jnp.concatenate([low, rest], axis=0)
            matrix = [jnp.concatenate([row_m[direction, level, 0, 0:count, :],
                                       row_m[direction, level, 1, 0:count, :]], axis=0)
                      for level in range(2)]
            made = dot3(matrix, (high, low))
            top, low_half = made[:count], made[count:]
            field = jnp.concatenate([top[:, :cols] - low_half[:, cols:],
                                     top[:, cols:] + low_half[:, :cols]], axis=1)
            made = dot3(split(field), (col_m[direction, 0], col_m[direction, 1]))
            return made[:, :cols], made[:, cols:]

        def start_halos(e, h):
            @pl.when(has_high)
            def _():
                halo_up(e, h).start()

            @pl.when(has_low)
            def _():
                halo_down(e, h).start()

        def take_halos(e, h):
            @pl.when(has_low)
            def _():
                halo_up(e, h).wait_recv()

            @pl.when(has_high)
            def _():
                halo_down(e, h).wait_recv()

        for s in range(1, slabs):
            par_send(s).wait_recv()
        local_par.start()
        local_par.wait()
        key, before = [], 0
        for s in range(slabs):
            number = par_s[s, 0, planes]
            for i in range(planes):
                key.append(jnp.where(i < number, before + i, -1))
            before = before + number
        total = slabs * planes
        may_be = [[p for p in range(total)
                   if 0 <= p - k <= min(total - live, (p // planes) * (planes - 1))]
                  for k in range(live)]
        shift = []
        for k in range(live):
            value = 0
            for p in may_be[k]:
                value = jnp.where(key[p] == k, par_s[p // planes, 0, p % planes], value)
            shift.append(value)

        ext = rows + 2 * edge
        at = lax.broadcasted_iota(jnp.int32, (ext, cols), 0) + (tile * rows - edge)
        inside = (at >= 0) & (at < tiles * rows)
        arrived = [0]

        def ready(slab_needed):
            while arrived[0] <= slab_needed:
                s = arrived[0]
                if s == 0:
                    local_ph.wait()
                else:
                    ph_mid(s).wait_recv()
                if edge:
                    @pl.when(has_low)
                    def _():
                        ph_up(s).wait_recv()

                    @pl.when(has_high)
                    def _():
                        ph_down(s).wait_recv()
                arrived[0] += 1

        def trig(k):
            ready(may_be[k][-1] // planes)
            value = None
            for p in may_be[k]:
                one = ph[p // planes, p % planes]
                value = one if value is None else jnp.where(key[p] == k, one, value)
            sine, cosine = sin_cos(value)
            sines[k] = jnp.where(inside, sine, 0.0)
            cosines[k] = jnp.where(inside, cosine, 0.0)

        local_inc.wait()
        k = 0
        for e, size in enumerate(fwd):
            h = size * STEP
            if e:
                start_halos(e, h)
            if e == len(fwd) - 1:
                build(1)
            for j in range(size):
                if j == 0:
                    trig(k)
                    take_halos(e, h)
                more = STEP * (size - 1 - j)
                count = rows + 2 * more
                real, imag = spread(fields[e] if j == 0 else mid.at[k], 8 + shift[k], count, 0)
                if j:
                    trig(k)
                sine = sines[k, edge - more:edge - more + count, :]
                cosine = cosines[k, edge - more:edge - more + count, :]
                new_r, new_i = real * cosine - imag * sine, real * sine + imag * cosine
                if j < size - 1:
                    mid[k + 1, 0, 0:count, :] = new_r
                    mid[k + 1, 1, 0:count, :] = new_i
                own_r, own_i = new_r[more:more + rows], new_i[more:more + rows]
                saved[k, 0], saved[k, 1] = own_r, own_i
                if j == size - 1 and e + 1 < len(fwd):
                    g = fwd[e + 1] * STEP
                    fields[e + 1][0, g:g + rows, :] = own_r
                    fields[e + 1][1, g:g + rows, :] = own_i
                k += 1

        local_aim.wait()
        slopes = {}
        last = live - 1
        adj_r, adj_i = own_r - aim[0], own_i - aim[1]

        def slope(k, adj_r, adj_i):
            slopes[k] = saved[k, 0] * adj_i - saved[k, 1] * adj_r

        def weigh(k, adj_r, adj_i, more):
            span = slice(edge - more, edge + rows + more)
            sine, cosine = sines[k, span, :], cosines[k, span, :]
            return adj_r * cosine + adj_i * sine, adj_i * cosine - adj_r * sine

        sent = [slabs]

        def hand_out(k):
            while sent[0] > 0:
                s = sent[0] - 1
                if min(kk for kk in range(live) for p in may_be[kk] if p // planes == s) < k:
                    return
                for i in range(planes):
                    p = s * planes + i
                    value = jnp.zeros((rows, cols), F32)
                    for kk in range(live):
                        if p in may_be[kk]:
                            value = jnp.where(key[p] == kk, slopes[kk], value)
                    if s:
                        grads[s, i] = value
                    else:
                        out[i] = value
                if s:
                    grad_send(s).start()
                sent[0] = s

        k = last
        for b, size in enumerate(bwd):
            e = len(fwd) + b
            h = size * STEP
            real, imag = weigh(k, adj_r, adj_i, 0)
            fields[e][0, h:h + rows, :] = real
            fields[e][1, h:h + rows, :] = imag
            start_halos(e, h)
            slope(k, adj_r, adj_i)
            hand_out(k)
            take_halos(e, h)
            for j in range(size):
                more = STEP * (size - 1 - j)
                count = rows + 2 * more
                real, imag = spread(fields[e] if j == 0 else mid.at[live + k], 8 - shift[k], count, 1)
                k -= 1
                if j < size - 1:
                    new_r, new_i = weigh(k, real, imag, more)
                    mid[live + k, 0, 0:count, :] = new_r
                    mid[live + k, 1, 0:count, :] = new_i
                adj_r, adj_i = real[more:more + rows], imag[more:more + rows]
                if j < size - 1:
                    slope(k, adj_r, adj_i)
                    hand_out(k)
        slope(0, adj_r, adj_i)
        hand_out(0)

        for e, size in enumerate(fwd + bwd):
            @pl.when(has_high)
            def _():
                (inc_up() if e == 0 else halo_up(e, size * STEP)).wait_send()

            @pl.when(has_low)
            def _():
                (inc_down() if e == 0 else halo_down(e, size * STEP)).wait_send()
        for s in range(1, slabs):
            grad_send(s).wait_send()

    if edge:
        @pl.when(has_high)
        def _():
            ph_up(slab).wait_send()

        @pl.when(has_low)
        def _():
            ph_down(slab).wait_send()

    @pl.when(jnp.logical_not(worker))
    def _():
        par_send(slab).wait_send()
        ph_mid(slab).wait_send()
        grad_send(slab).wait_recv()


def solution(mesh):
    tiles, slabs = mesh.shape["tile"], mesh.shape["slab"]

    def local(incident, target, kernel, phase_screen, plane_shift, slab_planes):
        planes, rows, cols = phase_screen.shape
        live = slabs * planes * 3 // 4
        fwd, bwd = groups_of(live), groups_of(live - 1)
        edge = (max(fwd + bwd) - 1) * STEP
        big = rows + 2 * edge
        wide = -(-(big + 2 * REACH) // 128) * 128
        n_ex = len(fwd) + len(bwd)
        cfg = (tiles, slabs, planes, rows, cols, live, fwd, bwd)
        dma = pltpu.SemaphoreType.DMA
        vmem = pltpu.VMEM
        scratch = [
            vmem((2, 2, 2, big, wide), BF16),
            vmem((2, 2, 2 * cols, 2 * cols), BF16),
            vmem((slabs, planes, big, cols), F32),
            vmem((slabs, 8, cols), jnp.int32),
            pltpu.SMEM((slabs, 8, cols), jnp.int32),
            vmem((live, big, cols), F32),
            vmem((live, big, cols), F32),
            vmem((live, 2, rows, cols), F32),
            vmem((2, rows, cols), F32),
            vmem((2 * live, 2, big, cols), F32),
            vmem((slabs, planes, rows, cols), F32),
            dma((4,)), dma, dma((slabs,)), dma((3,)), dma((slabs, 3)),
            dma((2 * n_ex,)), dma((2 * n_ex,)), dma((slabs,)), dma,
        ] + [vmem((2, rows + 2 * size * STEP, cols), F32) for size in fwd + bwd]
        smem = pl.BlockSpec(memory_space=pltpu.SMEM)
        hbm = pl.BlockSpec(memory_space=pl.ANY)
        return pl.pallas_call(
            functools.partial(body, cfg),
            out_shape=jax.ShapeDtypeStruct((planes, rows, cols), F32),
            in_specs=[smem, smem, smem, hbm, hbm, hbm],
            out_specs=pl.BlockSpec(memory_space=pltpu.VMEM),
            scratch_shapes=scratch,
            compiler_params=pltpu.CompilerParams(
                collective_id=0, has_side_effects=True, vmem_limit_bytes=48 * 2**20),
            name="diffraction",
        )(kernel, plane_shift, slab_planes, incident, target, phase_screen)

    placed = (P(None, "tile", None), P(None, "tile", None), P(), P("slab", "tile", None),
              P("slab"), P("slab"))
    return jax.shard_map(local, mesh=mesh, in_specs=placed,
                         out_specs=P("slab", "tile", None), check_vma=False)
```

time: 219 us -> 34.8 us (0.16)
  starting transfers between devices: 93.7 us -> 0 us
  waiting for transfers between devices: 71 us -> 0 us
  matrix products: 39.4 us -> 0 us
  Pallas kernels: 0 us -> 30.5 us
  other arithmetic: 8.58 us -> 0 us
    ppermute x36 -> x0, starting transfers between devices: 93.7 us -> none  [the longest x15 48.1 us: padded_2(): lax.ppermute(lax.slice_in_dim(block, block.shape[dim] - width, None, axis...]
    ppermute x36 -> x0, waiting for transfers between devices: 71 us -> none  [the longest x15 45.1 us: padded_2(): lax.ppermute(lax.slice_in_dim(block, 0, width, axis=dim), axis, backward)]
    dot_general x120 -> x0, matrix products: 39.4 us -> none  [product(): jnp.dot(left_side, right_side, precision=highest, preferred_element_type=...]
    pallas_call x0 -> x1, Pallas kernels: none -> 30.5 us  [local(): pl.pallas_call(functools.partial(body, cfg), out_shape=jax.ShapeDtypeStru...]
    reduce_sum x2 -> x0, other arithmetic: 3.12 us -> none  [the longest x1 2.35 us: tap_values(): real_part = jnp.sum(onehot * kernel[0], axis=-1)]
  transfers between devices with their start and end apart: 36 -> 0, of which waited for: 20 -> 0; matrix products, arithmetic and copies ran while one was open for 3% -> 0% of each run, Pallas kernels for 0% -> 0%
where the time goes in v1:
time: 34.8 us; the launch traced here: 34.5 us
  Pallas kernels  30.5 us (88%)
  local copies, waits for them, and re-layouts  3.37 us (10%)
  between operations  0.72 us (2%)
    pallas_call x1, Pallas kernels, local(): pl.pallas_call(functools.partial(body, cfg), out_shape=jax.ShapeDtypeStru...  30.5 us
    unnamed x11, local copies, waits for them, and re-layouts  3.37 us

profile of v1, /device:TPU:1, one launch (start us, length us, event | category | flops | bytes accessed | tf_op | source)
XLA Modules:
  0.0 34.5 jit_solution(12933202052325754695)
XLA Ops:
  0.0 0.0 copy-start.4
  0.0 0.0 copy-start.3
  0.7 0.0 copy-done.4
  0.7 0.0 copy-done.3
  0.7 0.0 copy-start
  0.7 0.9 %copy-done = f32[2,128,128]{2,1,0:T(8,128)S(1)} copy-done((f32[2,128,128]{2,1,0:T(8,128)S(1)}, f32[2,128,128]{2,1,0:T(8,128)}, u32[]{:S(2)}) %copy-start) | copy-done | bytes 131096
  1.6 0.0 copy-start.1
  1.6 0.9 %copy-done.1 = f32[2,128,128]{2,1,0:T(8,128)S(1)} copy-done((f32[2,128,128]{2,1,0:T(8,128)S(1)}, f32[2,128,128]{2,1,0:T(8,128)}, u32[]{:S(2)}) %copy-start.1) | copy-done | bytes 131096
  2.5 0.0 copy-start.2
  2.5 0.9 %copy-done.2 = f32[2,128,128]{2,1,0:T(8,128)S(1)} copy-done((f32[2,128,128]{2,1,0:T(8,128)S(1)}, f32[2,128,128]{2,1,0:T(8,128)}, u32[]{:S(2)}) %copy-start.2) | copy-done | bytes 131096
  3.4 30.5 %diffraction.1 = f32[2,128,128]{2,1,0:T(8,128)S(1)} custom-call(f32[2,33]{1,0:T(2,128)S(1)} %copy-done.3, s32[2]{0:T(128)S(1)} %copy-done.4, s32[1]{0:T(128)S(6)} %copy.8.counts, f32[2,128,128]{2,1,0:T(8,128)S(1)} %copy-done, f32[2,128,128]{2,1,0:T(8,128)S(1)} %copy-done.1, f32[2,128,128]{2,1,0:T(8,128)S(1)} %copy-done.2), custom_call_target="tpu_custom_call" | custom-call | tf_op jit(solution)/shard_map/diffraction/pallas_call | solution.py:452
  33.9 0.7 %copy.9 = f32[2,128,128]{2,1,0:T(8,128)} copy(f32[2,128,128]{2,1,0:T(8,128)S(1)} %diffraction.1) | data formatting | bytes 262144
Async XLA Ops:
  0.0 0.7 %copy-start.4 = (s32[2]{0:T(128)S(1)}, s32[2]{0:T(128)}, u32[]{:S(2)}) copy-start(s32[2]{0:T(128)} %shifts.1) | copy-start | bytes 28
  0.0 0.7 %copy-start.3 = (f32[2,33]{1,0:T(2,128)S(1)}, f32[2,33]{1,0:T(2,128)}, u32[]{:S(2)}) copy-start(f32[2,33]{1,0:T(2,128)} %taps.1) | copy-start | bytes 796
  0.7 0.9 %copy-start = (f32[2,128,128]{2,1,0:T(8,128)S(1)}, f32[2,128,128]{2,1,0:T(8,128)}, u32[]{:S(2)}) copy-start(f32[2,128,128]{2,1,0:T(8,128)} %incident.1) | copy-start | bytes 393220
  1.6 0.9 %copy-start.1 = (f32[2,128,128]{2,1,0:T(8,128)S(1)}, f32[2,128,128]{2,1,0:T(8,128)}, u32[]{:S(2)}) copy-start(f32[2,128,128]{2,1,0:T(8,128)} %target.1) | copy-start | bytes 393220
  2.5 0.9 %copy-start.2 = (f32[2,128,128]{2,1,0:T(8,128)S(1)}, f32[2,128,128]{2,1,0:T(8,128)}, u32[]{:S(2)}) copy-start(f32[2,128,128]{2,1,0:T(8,128)} %phases.1) | copy-start | bytes 393220

commit v2 on v1

--- a/solution.py
+++ b/solution.py
@@ -11,15 +11,15 @@
 TILT_MAX = 8
 REACH = 16
 STEP = REACH + TILT_MAX
-DEPTH = 3
+AHEAD, BACK = 3, 3
 MESH = pl.DeviceIdType.MESH
 F32, BF16 = jnp.float32, jnp.bfloat16
 
 
-def groups_of(count):
-    out = [DEPTH] * (count // DEPTH)
-    if count % DEPTH:
-        out.append(count % DEPTH)
+def groups_of(count, depth):
+    out = [depth] * (count // depth)
+    if count % depth:
+        out.append(count % depth)
     return out
 
 
@@ -45,10 +45,10 @@
 
 
 def body(cfg, taps, shifts, counts, incident, target, phases, out, *scratch):
-    tiles, slabs, planes, rows, cols, live, fwd, bwd = cfg
+    tiles, slabs, planes, rows, cols, live, fwd, bwd, may_be, need, gated = cfg
     n_ex = len(fwd) + len(bwd)
     (row_m, col_m, ph, par, par_s, sines, cosines, saved, aim, mid, grads,
-     own_sem, par_ssem, par_rsem, ph_ssem, ph_rsem, ex_ssem, ex_rsem, g_ssem, g_rsem,
+     own_sem, par_ssem, par_rsem, ph_ssem, ph_rsem, ex_ssem, ex_rsem, g_ssem, g_rsem, go_sem, ed_ssem, ed_rsem,
      *fields) = scratch
     edge = ph.shape[2] - rows
     edge //= 2
@@ -104,15 +104,17 @@
 
     def ph_mid(s):
         return remote(phases, ph.at[s, :, edge:edge + rows, :],
-                      ph_ssem.at[0], ph_rsem.at[s, 0], tile, 0)
-
-    def ph_up(s):
-        return remote(phases.at[:, rows - edge:, :], ph.at[s, :, 0:edge, :],
-                      ph_ssem.at[1], ph_rsem.at[s, 1], tile + 1, 0)
-
-    def ph_down(s):
-        return remote(phases.at[:, 0:edge, :], ph.at[s, :, edge + rows:, :],
-                      ph_ssem.at[2], ph_rsem.at[s, 2], tile - 1, 0)
+                      ph_ssem, ph_rsem.at[s], tile, 0)
+
+    def ph_up(p):
+        s, i, w = p // planes, p % planes, need[p]
+        return remote(phases.at[i, rows - w:, :], ph.at[s, i, edge - w:edge, :],
+                      ed_ssem.at[i, 0], ed_rsem.at[p, 0], tile + 1, 0)
+
+    def ph_down(p):
+        s, i, w = p // planes, p % planes, need[p]
+        return remote(phases.at[i, 0:w, :], ph.at[s, i, edge + rows:edge + rows + w, :],
+                      ed_ssem.at[i, 1], ed_rsem.at[p, 1], tile - 1, 0)
 
     def par_send(s):
         return remote(par.at[s], par.at[s], par_ssem, par_rsem.at[s], tile, 0)
@@ -130,6 +132,7 @@
     local_inc = pltpu.make_async_copy(incident, fields[0].at[:, h0:h0 + rows, :], own_sem.at[0])
     local_ph = pltpu.make_async_copy(phases, ph.at[0, :, edge:edge + rows, :], own_sem.at[1])
     local_aim = pltpu.make_async_copy(target, aim, own_sem.at[2])
+    local_out = pltpu.make_async_copy(grads.at[0], out, own_sem.at[4])
     local_par = pltpu.make_async_copy(par, par_s, own_sem.at[3])
 
     greeters = has_low.astype(jnp.int32) + has_high.astype(jnp.int32)
@@ -148,14 +151,27 @@
         par_send(slab).start()
         ph_mid(slab).start()
 
-    if edge:
-        @pl.when(has_high)
-        def _():
-            ph_up(slab).start()
-
-        @pl.when(has_low)
-        def _():
-            ph_down(slab).start()
+    def on_edges(list_of_planes, act):
+        if list_of_planes:
+            @pl.when(has_high)
+            def _():
+                for p in list_of_planes:
+                    act(ph_up(p))
+
+            @pl.when(has_low)
+            def _():
+                for p in list_of_planes:
+                    act(ph_down(p))
+
+    edged = [[p for p in range(s * planes, (s + 1) * planes) if need[p]] for s in range(slabs)]
+    for s in range(slabs):
+        @pl.when(slab == s)
+        def _(s=s):
+            on_edges([p for p in edged[s] if p not in gated], lambda copy: copy.start())
+            later = [p for p in edged[s] if p in gated]
+            if later:
+                pl.semaphore_wait(go_sem, 1)
+                on_edges(later, lambda copy: copy.start())
 
     @pl.when(worker)
     def _():
@@ -256,10 +272,6 @@
             for i in range(planes):
                 key.append(jnp.where(i < number, before + i, -1))
             before = before + number
-        total = slabs * planes
-        may_be = [[p for p in range(total)
-                   if 0 <= p - k <= min(total - live, (p // planes) * (planes - 1))]
-                  for k in range(live)]
         shift = []
         for k in range(live):
             value = 0
@@ -270,34 +282,53 @@
         ext = rows + 2 * edge
         at = lax.broadcasted_iota(jnp.int32, (ext, cols), 0) + (tile * rows - edge)
         inside = (at >= 0) & (at < tiles * rows)
-        arrived = [0]
-
-        def ready(slab_needed):
-            while arrived[0] <= slab_needed:
-                s = arrived[0]
-                if s == 0:
-                    local_ph.wait()
-                else:
-                    ph_mid(s).wait_recv()
-                if edge:
+        have_mid, have_edge = set(), set()
+
+        def ready(some, mids, edges):
+            for p in some:
+                s = p // planes
+                if mids and s not in have_mid:
+                    have_mid.add(s)
+                    if s == 0:
+                        local_ph.wait()
+                    else:
+                        ph_mid(s).wait_recv()
+                if edges and need[p] and p not in have_edge:
+                    have_edge.add(p)
+
                     @pl.when(has_low)
                     def _():
-                        ph_up(s).wait_recv()
+                        ph_up(p).wait_recv()
 
                     @pl.when(has_high)
                     def _():
-                        ph_down(s).wait_recv()
-                arrived[0] += 1
-
-        def trig(k):
-            ready(may_be[k][-1] // planes)
+                        ph_down(p).wait_recv()
+
+        def trig(k, low, high):
+            ready(may_be[k], high > 0 and low < rows,
+                  low < 0 or high > rows)
+            span = slice(edge + low, edge + high)
             value = None
             for p in may_be[k]:
-                one = ph[p // planes, p % planes]
+                one = ph[p // planes, p % planes, span, :]
                 value = one if value is None else jnp.where(key[p] == k, one, value)
             sine, cosine = sin_cos(value)
-            sines[k] = jnp.where(inside, sine, 0.0)
-            cosines[k] = jnp.where(inside, cosine, 0.0)
+            if low < 0 or high > rows:
+                sine = jnp.where(inside[span], sine, 0.0)
+                cosine = jnp.where(inside[span], cosine, 0.0)
+            sines[k, span, :] = sine
+            cosines[k, span, :] = cosine
+
+        known = {}
+
+        def widen(k, more):
+            if k not in known:
+                trig(k, -more, rows + more)
+                known[k] = more
+            elif known[k] < more:
+                trig(k, -more, -known[k])
+                trig(k, rows + known[k], rows + more)
+                known[k] = more
 
         local_inc.wait()
         k = 0
@@ -308,14 +339,18 @@
             if e == len(fwd) - 1:
                 build(1)
             for j in range(size):
+                more = STEP * (size - 1 - j)
                 if j == 0:
-                    trig(k)
+                    if e:
+                        widen(k, more)
                     take_halos(e, h)
-                more = STEP * (size - 1 - j)
+                    if e == 0:
+                        for s in sorted({p // planes for p in gated}):
+                            pl.semaphore_signal(go_sem, inc=1, device_id={"tile": tile, "slab": s},
+                                                device_id_type=MESH)
                 count = rows + 2 * more
                 real, imag = spread(fields[e] if j == 0 else mid.at[k], 8 + shift[k], count, 0)
-                if j:
-                    trig(k)
+                widen(k, more)
                 sine = sines[k, edge - more:edge - more + count, :]
                 cosine = cosines[k, edge - more:edge - more + count, :]
                 new_r, new_i = real * cosine - imag * sine, real * sine + imag * cosine
@@ -356,12 +391,12 @@
                     for kk in range(live):
                         if p in may_be[kk]:
                             value = jnp.where(key[p] == kk, slopes[kk], value)
-                    if s:
-                        grads[s, i] = value
-                    else:
-                        out[i] = value
+                    grads[s, i] = value
                 if s:
                     grad_send(s).start()
+                else:
+                    local_out.start()
+                    local_out.wait()
                 sent[0] = s
 
         k = last
@@ -374,6 +409,8 @@
             start_halos(e, h)
             slope(k, adj_r, adj_i)
             hand_out(k)
+            for j in range(size - 1):
+                widen(k - 1 - j, STEP * (size - 1 - j))
             take_halos(e, h)
             for j in range(size):
                 more = STEP * (size - 1 - j)
@@ -391,6 +428,7 @@
         slope(0, adj_r, adj_i)
         hand_out(0)
 
+        ready(range(slabs * planes), True, True)
         for e, size in enumerate(fwd + bwd):
             @pl.when(has_high)
             def _():
@@ -402,14 +440,10 @@
         for s in range(1, slabs):
             grad_send(s).wait_send()
 
-    if edge:
-        @pl.when(has_high)
-        def _():
-            ph_up(slab).wait_send()
-
-        @pl.when(has_low)
-        def _():
-            ph_down(slab).wait_send()
+    for s in range(slabs):
+        @pl.when(slab == s)
+        def _(s=s):
+            on_edges(edged[s], lambda copy: copy.wait_send())
 
     @pl.when(jnp.logical_not(worker))
     def _():
@@ -424,12 +458,31 @@
     def local(incident, target, kernel, phase_screen, plane_shift, slab_planes):
         planes, rows, cols = phase_screen.shape
         live = slabs * planes * 3 // 4
-        fwd, bwd = groups_of(live), groups_of(live - 1)
+        fwd, bwd = groups_of(live, AHEAD), groups_of(live - 1, BACK)
         edge = (max(fwd + bwd) - 1) * STEP
         big = rows + 2 * edge
         wide = -(-(big + 2 * REACH) // 128) * 128
         n_ex = len(fwd) + len(bwd)
-        cfg = (tiles, slabs, planes, rows, cols, live, fwd, bwd)
+        total = slabs * planes
+        may_be = [[p for p in range(total)
+                   if 0 <= p - k <= min(total - live, (p // planes) * (planes - 1))]
+                  for k in range(live)]
+        used = [0] * live
+        k = 0
+        for size in fwd:
+            for j in range(size):
+                used[k] = STEP * (size - 1 - j)
+                k += 1
+        k = live - 1
+        for size in bwd:
+            for j in range(size):
+                k -= 1
+                if j < size - 1:
+                    used[k] = max(used[k], STEP * (size - 1 - j))
+        need = [max(used[k] for k in range(live) if p in may_be[k]) for p in range(total)]
+        gated = [p for p in range(planes, total) if need[p] and
+                 min(k for k in range(live) if p in may_be[k] and used[k]) >= fwd[0]]
+        cfg = (tiles, slabs, planes, rows, cols, live, fwd, bwd, may_be, need, gated)
         dma = pltpu.SemaphoreType.DMA
         vmem = pltpu.VMEM
         scratch = [
@@ -444,8 +497,9 @@
             vmem((2, rows, cols), F32),
             vmem((2 * live, 2, big, cols), F32),
             vmem((slabs, planes, rows, cols), F32),
-            dma((4,)), dma, dma((slabs,)), dma((3,)), dma((slabs, 3)),
-            dma((2 * n_ex,)), dma((2 * n_ex,)), dma((slabs,)), dma,
+            dma((5,)), dma, dma((slabs,)), dma, dma((slabs,)),
+            dma((2 * n_ex,)), dma((2 * n_ex,)), dma((slabs,)), dma, pltpu.SemaphoreType.REGULAR,
+            dma((planes, 2)), dma((slabs * planes, 2)),
         ] + [vmem((2, rows + 2 * size * STEP, cols), F32) for size in fwd + bwd]
         smem = pl.BlockSpec(memory_space=pltpu.SMEM)
         hbm = pl.BlockSpec(memory_space=pl.ANY)
@@ -453,10 +507,10 @@
             functools.partial(body, cfg),
             out_shape=jax.ShapeDtypeStruct((planes, rows, cols), F32),
             in_specs=[smem, smem, smem, hbm, hbm, hbm],
-            out_specs=pl.BlockSpec(memory_space=pltpu.VMEM),
+            out_specs=pl.BlockSpec(memory_space=pl.ANY),
             scratch_shapes=scratch,
             compiler_params=pltpu.CompilerParams(
-                collective_id=0, has_side_effects=True, vmem_limit_bytes=48 * 2**20),
+                collective_id=0, has_side_effects=True, vmem_limit_bytes=55040 * 2**10),
             name="diffraction",
         )(kernel, plane_shift, slab_planes, incident, target, phase_screen)
 

time: 34.8 us -> 30.2 us (0.87)
  local copies, waits for them, and re-layouts: 3.37 us -> 0.67 us
  Pallas kernels: 30.5 us -> 28.5 us
    unnamed x11 -> x5, local copies, waits for them, and re-layouts: 3.37 us -> 0.67 us
    pallas_call x1, Pallas kernels: 30.5 us -> 28.5 us  [local(): pl.pallas_call(functools.partial(body, cfg), out_shape=jax.ShapeDtypeStru...]
where the time goes in v2:
time: 30.2 us; the launch traced here: 29.8 us
  Pallas kernels  28.5 us (94%)
  between operations  0.7 us (2%)
  local copies, waits for them, and re-layouts  0.67 us (2%)
    pallas_call x1, Pallas kernels, local(): pl.pallas_call(functools.partial(body, cfg), out_shape=jax.ShapeDtypeStru...  28.5 us
    unnamed x5, local copies, waits for them, and re-layouts  0.67 us

profile of v2, /device:TPU:1, one launch (start us, length us, event | category | flops | bytes accessed | tf_op | source)
XLA Modules:
  0.0 29.8 jit_solution(18014813870738806454)
XLA Ops:
  0.0 0.0 copy-start.1
  0.0 0.0 copy-start
  0.7 0.0 copy-done.1
  0.7 0.0 copy-done
  0.7 28.5 %diffraction.1 = f32[2,128,128]{2,1,0:T(8,128)S(1)} custom-call(f32[2,33]{1,0:T(2,128)S(1)} %copy-done, s32[2]{0:T(128)S(1)} %copy-done.1, s32[1]{0:T(128)S(6)} %copy.8.counts, f32[2,128,128]{2,1,0:T(8,128)} %incident.1, f32[2,128,128]{2,1,0:T(8,128)} %target.1, f32[2,128,128]{2,1,0:T(8,128)} %phases.1), custom_call_target="tpu_custom_call" | custom-call | tf_op jit(solution)/shard_map/diffraction/pallas_call | solution.py:506
  29.2 0.7 %copy.9 = f32[2,128,128]{2,1,0:T(8,128)} copy(f32[2,128,128]{2,1,0:T(8,128)S(1)} %diffraction.1) | data formatting | bytes 262144
Async XLA Ops:
  0.0 0.7 %copy-start.1 = (s32[2]{0:T(128)S(1)}, s32[2]{0:T(128)}, u32[]{:S(2)}) copy-start(s32[2]{0:T(128)} %shifts.1) | copy-start | bytes 28
  0.0 0.7 %copy-start = (f32[2,33]{1,0:T(2,128)S(1)}, f32[2,33]{1,0:T(2,128)}, u32[]{:S(2)}) copy-start(f32[2,33]{1,0:T(2,128)} %taps.1) | copy-start | bytes 796
